TPU v7x, 512 devices: a whole 4x4x16 slice. The times are simulated.
512 devices in a mesh: dp: 32 (over z_lo, x), tensor: 16 (over y, z_hi, core).
Axes of the slice: x: 4, y: 4, z: 16 (z_hi: 2, z_lo: 8; z = z_hi * 8 + z_lo), core: 2. Of those that a mesh axis runs over, the one named last changes fastest.
Arguments:
- x_panel: bfloat16 [16384, 4096], P('dp', 'tensor'), may hold values from -6 to 6
- grad_hidden: bfloat16 [16384, 14336], P('dp', 'tensor'), may hold values from -0.046875 to 0.046875
- gate_blocks: bfloat16 [112, 8, 128, 128], P('tensor'), may hold values from -0.1875 to 0.1875
- up_blocks: bfloat16 [112, 8, 128, 128], P('tensor'), may hold values from -0.1875 to 0.1875
- block_rows: int32 [112, 8], P('tensor'), may hold values from 0 to 31, as said below
- block_owner: int32 [112, 8], P('tensor'), may hold values from 0 to 31, as said below
Outputs:
- grad_owned: float32 [16, 32, 2, 2, 128, 128], P('tensor', 'dp')
Inputs may be any that keep to these rules, and one draw needn't show every extreme that they name: `block_rows`: the 8 block rows of one block column are distinct. `block_owner`: within each group of 7 consecutive block columns every dp index owns at most 2 blocks, and some index owns exactly 2.
All inputs are finite; a program needn't handle non-finite values.
Results may differ from a plain program's by a relative error of at most 0.013.
Values may be sent and summed in bfloat16 or wider, within the bound.
No kernel may reach another device: no remote copies, remote signals or barrier semaphores. Data moves between devices by JAX's collectives and lax.ppermute only.
A program may use at most 64 MiB of HBM per device.

v0:
```python
import jax
import jax.numpy as jnp
from jax import lax
from jax.sharding import PartitionSpec as P


def silu_parts(gate_pre):
    sigmoid_v = jax.nn.sigmoid(gate_pre)
    return (gate_pre * sigmoid_v, sigmoid_v * (1.0 + gate_pre * (1.0 - sigmoid_v)))


def body(x_panel, grad_hidden, gate_blocks, up_blocks, block_rows, block_owner):
    gathered = lax.all_gather(x_panel, "tensor", axis=1, tiled=True)
    token_count = gathered.shape[0]
    column_count = gate_blocks.shape[0]
    depth = gate_blocks.shape[1]
    block_size = gate_blocks.shape[2]
    row_total = gathered.shape[1] // block_size
    picked = gathered.reshape(token_count, row_total, block_size)[:, block_rows, :]
    gate_pre = jnp.einsum("tckb,ckbe->tce", picked, gate_blocks, preferred_element_type=jnp.float32)
    up_pre = jnp.einsum("tckb,ckbe->tce", picked, up_blocks, preferred_element_type=jnp.float32)
    activation, derivative = silu_parts(gate_pre)
    grad_f32 = grad_hidden.reshape(token_count, column_count, block_size).astype(jnp.float32)
    grad_gate_act = (grad_f32 * up_pre * derivative).astype(jnp.bfloat16)
    grad_up_act = (grad_f32 * activation).astype(jnp.bfloat16)
    paired = jnp.stack([grad_gate_act, grad_up_act], 2)
    partial_value = jnp.einsum(
        "tckb,tcme->ckmbe", picked, paired, preferred_element_type=jnp.float32
    )
    partial_value = partial_value.astype(jnp.bfloat16)
    owner_count = lax.axis_size("dp")
    block_count = column_count * depth
    capacity = block_count // owner_count + 1
    flat_owner = block_owner.reshape(block_count)
    onehot = (flat_owner[:, None] == jnp.arange(owner_count, dtype=jnp.int32)[None, :]).astype(
        jnp.int32
    )
    before = jnp.cumsum(onehot, 0) - onehot
    slot_index = jnp.sum(onehot * before, 1)
    target = flat_owner * capacity + slot_index
    packed = jnp.zeros((owner_count * capacity, 2, block_size, block_size), jnp.bfloat16)
    packed = packed.at[target].set(partial_value.reshape(block_count, 2, block_size, block_size))
    arrived = lax.all_to_all(
        packed.reshape(owner_count, capacity, 2, block_size, block_size),
        "dp",
        split_axis=0,
        concat_axis=0,
        tiled=True,
    )
    summed = jnp.sum(arrived.astype(jnp.float32), 0)
    return summed.reshape(1, 1, capacity, 2, block_size, block_size)


def solution(mesh):
    in_specs = (
        P("dp", "tensor"),
        P("dp", "tensor"),
        P("tensor", None, None, None),
        P("tensor", None, None, None),
        P("tensor", None),
        P("tensor", None),
    )
    out_specs = P("tensor", "dp", None, None, None, None)
    return jax.shard_map(body, mesh=mesh, in_specs=in_specs, out_specs=out_specs, check_vma=False)
```

profile of v0, /device:TPU:8, one launch (start us, length us, event | category | flops | bytes accessed | tf_op | source)
XLA Modules:
  0.0 384.3 jit_solution(14458488507015758200)
XLA Ops:
  6.5 0.0 copy-start
  6.5 0.0 all-gather.2.cloned.1.call-start
  6.5 1.9 copy.22
  8.5 0.0 all-gather.2.cloned.1.call-update
  8.5 0.7 compare_select_fusion
  9.2 0.1 reshape.52
  9.3 1.5 copy.21
  10.7 0.0 copy-start.3
  10.7 1.6 copy.24
  12.3 0.0 copy-done.3
  12.3 0.1 eq.15
  12.4 0.1 mul.39
  12.5 0.1 fusion.12
  12.6 0.1 reduce_window_sum.11
  12.7 0.2 select_reduce_fusion
  12.9 120.1 %all-gather.2.cloned.1.call-done = bf16[512,4096]{0,1:T(8,128)(2,1)} async-done(((bf16[512,256]{0,1:T(8,128)(2,1)}), bf16[512,4096]{0,1:T(8,128)(2,1)}) %all-gather.2.cloned.1.call-update) | async-done | bytes 4194320 | tf_op jit(solution)/shard_map/all_gather | solution.py:13
  132.9 6.4 %copy.23 = bf16[512,32,128]{2,0,1:T(8,128)(2,1)} copy(bf16[512,32,128]{0,2,1:T(8,128)(2,1)} %bitcast.81) | data formatting | bytes 8388608 | tf_op jit(solution)/shard_map/reshape | solution.py:19
  139.4 7.4 %gather_fusion = bf16[56,512,128]{2,1,0:T(8,128)(2,1)} fusion(bf16[512,32,128]{2,0,1:T(8,128)(2,1)} %copy.23, s32[1024]{0:T(1024)S(1)} %pad_clamp_fusion), kind=kCustom, calls=%fused_computation | custom fusion | bytes 14680288 | tf_op jit(solution)/shard_map/gather | solution.py:19
  146.8 0.0 copy-done
  146.8 0.0 copy-start.1
  146.9 0.0 copy-start.2
  146.9 5.3 %fusion.14 = f32[7,512,128,1]{2,1,3,0:T(8,128)S(1)} fusion(bf16[512,7,8,128]{3,0,2,1:T(8,128)(2,1)} %bitcast.78, bf16[7,8,128,128]{3,2,1,0:T(8,128)(2,1)S(1)} %copy-done), kind=kOutput, calls=%fused_computation.30 | convolution fusion | flops 939524096 | bytes 11010048 | tf_op jit(solution)/shard_map/tckb,ckbe->tce/dot_general | solution.py:20
  152.1 0.0 copy-done.1
  152.2 0.0 copy-start.4
  152.2 0.5 fusion.11
  152.7 0.0 copy-done.2
  152.7 1.1 copy-done.4
  153.8 2.1 fusion.10
  155.9 3.9 %convert_bitcast_fusion = bf16[7,8,2,128,128]{3,4,1,2,0:T(8,128)(2,1)} fusion(bf16[512,7,8,128,1]{3,0,2,4,1:T(8,128)(2,1)S(1)} %bitcast.80, bf16[512,7,1,128]{3,0,1,2:T(8,128)(2,1)S(1)} %fusion.11, bf16[512,7,1,128]{3,0,1,2:T(8,128)(2,1)S(1)} %fusion.10), kind=kOutput, calls=%fused_computation.3 | convolution fusion | flops 1881800704 | bytes 12845056 | tf_op jit(solution)/shard_map/tckb,tcme->ckmbe/dot_general | solution.py:27
  159.8 6.2 %copy.27 = bf16[7,8,2,128,128]{4,3,2,1,0:T(8,128)(2,1)} copy(bf16[7,8,2,128,128]{3,4,1,2,0:T(8,128)(2,1)} %convert_bitcast_fusion) | data formatting | bytes 7340032 | tf_op jit(solution)/shard_map/convert_element_type | solution.py:30
  166.0 3.0 broadcast_in_dim.8
  169.0 11.6 %scatter_fusion = bf16[64,2,128,128]{3,2,1,0:T(8,128)(2,1)} fusion(bf16[64,2,128,128]{3,2,1,0:T(8,128)(2,1)} %broadcast_in_dim.8, s32[56]{0:T(128)S(1)} %fusion.13, bf16[56,2,128,128]{3,2,1,0:T(8,128)(2,1)} %bitcast.77), kind=kCustom, calls=%fused_computation.1 | custom fusion | bytes 11010272 | tf_op jit(solution)/shard_map/scatter | solution.py:42
  180.6 195.5 %all_to_all.5 = bf16[32,2,2,128,128]{4,3,2,1,0:T(8,128)(2,1)S(1)} all-to-all(bf16[32,2,2,128,128]{4,3,2,1,0:T(8,128)(2,1)} %bitcast.76), channel_id=1, replica_groups=mesh['dp'=32,'tensor'=16] {'dp'}, dimensions={0} | all-to-all | bytes 8388608 | tf_op jit(solution)/shard_map/all_to_all | solution.py:43
  376.0 1.5 convert_reduce_fusion
  (3 shorter events, 0.0 us)
Async XLA Ops:
  6.5 140.3 %copy-start = (bf16[7,8,128,128]{3,2,1,0:T(8,128)(2,1)S(1)}, bf16[7,8,128,128]{3,2,1,0:T(8,128)(2,1)}, u32[]{:S(2)}) copy-start(bf16[7,8,128,128]{3,2,1,0:T(8,128)(2,1)} %param.8) | copy-start | bytes 5505028
  6.5 126.4 %all-gather.2.cloned.1.call-start = ((), (), s32[]{:S(2)}) async-start(), calls=%async_computation.1 | async-start | bytes 4456448 | tf_op jit(solution)/shard_map/all_gather | solution.py:13
  10.7 1.6 copy-start.3
  146.8 5.3 %copy-start.1 = (f32[512,7,128]{2,0,1:T(8,128)S(1)}, f32[512,7,128]{2,0,1:T(8,128)}, u32[]{:S(2)}) copy-start(f32[512,7,128]{2,0,1:T(8,128)} %copy.24) | copy-start | bytes 5505028
  146.9 5.8 %copy-start.2 = (bf16[56,512,128]{2,1,0:T(8,128)(2,1)S(1)}, bf16[56,512,128]{2,1,0:T(8,128)(2,1)}, u32[]{:S(2)}) copy-start(bf16[56,512,128]{2,1,0:T(8,128)(2,1)} %gather_fusion) | copy-start | bytes 22020100
  152.2 1.6 copy-start.4
Sparse Core Ops, SparseCore 0:
  10.6 122.2 all-gather.1
where the time goes:
time: 385 us; the launch traced here: 384 us
  blocking collectives  195 us (51%)
  waiting for transfers between devices  120 us (31%)
  local copies, waits for them, and re-layouts  41 us (11%)
  between operations  13.5 us (4%)
  matrix products  11.3 us (3%)
    all_to_all x1, blocking collectives, body(): lax.all_to_all(packed.reshape(owner_count, capacity, 2, block_size, block...  195 us
    all_gather x1, waiting for transfers between devices, body(): gathered = lax.all_gather(x_panel, 'tensor', axis=1, tiled=True)  120 us
    scatter x1, local copies, waits for them, and re-layouts, body(): packed.at[target]  11.6 us
  transfers between devices with their start and end apart: 1, of which 1 were waited for; matrix products, arithmetic and copies ran while one was open for 1% of the time, Pallas kernels for 0%

commit v1 on v0

--- a/solution.py
+++ b/solution.py
@@ -10,7 +10,9 @@
 
 
 def body(x_panel, grad_hidden, gate_blocks, up_blocks, block_rows, block_owner):
-    gathered = lax.all_gather(x_panel, "tensor", axis=1, tiled=True)
+    gathered = jnp.concatenate(
+        lax.all_to_all(jnp.stack([x_panel] * lax.axis_size("tensor")), "tensor", 0, 0), axis=1
+    )
     token_count = gathered.shape[0]
     column_count = gate_blocks.shape[0]
     depth = gate_blocks.shape[1]

time: 385 us -> 471 us (1.22)
  blocking collectives: 195 us -> 323 us
  waiting for transfers between devices: 120 us -> 73.2 us
  starting transfers between devices: 0.01 us -> 18.3 us
  between operations: 13.5 us -> 0.11 us
    all_to_all x1, blocking collectives: 195 us -> 323 us  [body(): lax.all_to_all(packed.reshape(owner_count, capacity, 2, block_size, block...]
    all_gather x1 -> x0, waiting for transfers between devices: 120 us -> none  [body(): gathered = lax.all_gather(x_panel, 'tensor', axis=1, tiled=True)]
    all_to_all x0 -> x1, waiting for transfers between devices: none -> 73.2 us  [body(): lax.all_to_all(jnp.stack([x_panel] * lax.axis_size('tensor')), 'tensor',...]
    all_to_all x0 -> x1, starting transfers between devices: none -> 18.3 us  [body(): lax.all_to_all(jnp.stack([x_panel] * lax.axis_size('tensor')), 'tensor',...]
    another operation x0 -> x2, local copies, waits for them, and re-layouts: none -> 8.83 us  [the longest x1 6.45 us: body(): gathered.reshape(token_count, row_total, block_size)[:, block_rows, :]]
    reshape x1 -> x0, local copies, waits for them, and re-layouts: 6.45 us -> none  [body(): gathered.reshape(token_count, row_total, block_size)[:, block_rows, :]]
where the time goes in v1:
time: 471 us; the launch traced here: 470 us
  blocking collectives  323 us (69%)
  waiting for transfers between devices  73.2 us (16%)
  local copies, waits for them, and re-layouts  42.7 us (9%)
  starting transfers between devices  18.3 us (4%)
  matrix products  11.3 us (2%)
    all_to_all x1, blocking collectives, body(): lax.all_to_all(packed.reshape(owner_count, capacity, 2, block_size, block...  323 us
    all_to_all x1, waiting for transfers between devices, body(): lax.all_to_all(jnp.stack([x_panel] * lax.axis_size('tensor')), 'tensor',...  73.2 us
    all_to_all x1, starting transfers between devices, body(): lax.all_to_all(jnp.stack([x_panel] * lax.axis_size('tensor')), 'tensor',...  18.3 us
    scatter x1, local copies, waits for them, and re-layouts, body(): packed.at[target]  11.6 us
  transfers between devices with their start and end apart: 1, of which 1 were waited for; matrix products, arithmetic and copies ran while one was open for 1% of the time, Pallas kernels for 0%

profile of v1, /device:TPU:8, one launch (start us, length us, event | category | flops | bytes accessed | tf_op | source)
XLA Modules:
  0.0 470.5 jit_solution(4421788211905937213)
XLA Ops:
  0.0 0.0 copy-start
  0.0 1.2 copy.16
  1.2 2.4 stack.8
  3.6 0.0 copy-start.4
  3.6 18.3 %all-to-all-start = ((bf16[16,512,256]{1,2,0:T(8,128)(2,1)}), bf16[16,512,256]{1,2,0:T(8,128)(2,1)}, u32[]{:S(2)}, u32[]{:S(2)}) async-start(bf16[16,512,256]{1,2,0:T(8,128)(2,1)} %stack.8), calls=%async_computation | async-start | bytes 8388608 | tf_op jit(solution)/shard_map/all_to_all | solution.py:14
  21.9 0.0 copy-done.4
  21.9 0.1 reshape.54
  22.0 1.5 copy.15
  23.5 0.0 copy-start.3
  23.5 1.6 copy.18
  25.1 0.0 copy-done.3
  25.1 0.1 eq.15
  25.2 0.1 mul.39
  25.3 0.1 fusion.12
  25.3 0.1 reduce_window_sum.11
  25.4 0.2 select_reduce_fusion
  25.6 73.2 %all-to-all-done = bf16[16,512,256]{1,2,0:T(8,128)(2,1)} async-done(((bf16[16,512,256]{1,2,0:T(8,128)(2,1)}), bf16[16,512,256]{1,2,0:T(8,128)(2,1)}, u32[]{:S(2)}, u32[]{:S(2)}) %all-to-all-start) | async-done | bytes 4194336 | tf_op jit(solution)/shard_map/all_to_all | solution.py:14
  98.8 6.5 %copy.17 = bf16[512,32,128]{2,0,1:T(8,128)(2,1)} copy(bf16[512,32,128]{0,2,1:T(8,128)(2,1)} %bitcast.4) | data formatting | bytes 8388608 | tf_op jit(solution)/shard_map/reshape;reshape | solution.py:21
  105.3 7.4 %gather_fusion = bf16[56,512,128]{2,1,0:T(8,128)(2,1)} fusion(bf16[512,32,128]{2,0,1:T(8,128)(2,1)} %copy.17, s32[1024]{0:T(1024)S(1)} %pad_clamp_fusion), kind=kCustom, calls=%fused_computation | custom fusion | bytes 14680288 | tf_op jit(solution)/shard_map/gather | solution.py:21
  112.7 0.0 copy-done
  112.7 0.0 copy-start.1
  112.7 0.0 copy-start.2
  112.7 5.3 %fusion.14 = f32[7,512,128,1]{2,1,3,0:T(8,128)S(1)} fusion(bf16[512,7,8,128]{3,0,2,1:T(8,128)(2,1)} %bitcast.80, bf16[7,8,128,128]{3,2,1,0:T(8,128)(2,1)S(1)} %copy-done), kind=kOutput, calls=%fused_computation.30 | convolution fusion | flops 939524096 | bytes 11010048 | tf_op jit(solution)/shard_map/tckb,ckbe->tce/dot_general | solution.py:22
  118.0 0.0 copy-done.1
  118.0 0.0 copy-start.5
  118.0 0.5 fusion.11
  118.5 0.0 copy-done.2
  118.5 1.1 copy-done.5
  119.6 2.1 fusion.10
  121.8 3.9 convert_bitcast_fusion
  125.7 6.2 %copy.21 = bf16[7,8,2,128,128]{4,3,2,1,0:T(8,128)(2,1)} copy(bf16[7,8,2,128,128]{3,4,1,2,0:T(8,128)(2,1)} %convert_bitcast_fusion) | data formatting | bytes 7340032 | tf_op jit(solution)/shard_map/convert_element_type | solution.py:32
  131.9 3.0 broadcast_in_dim.8
  134.9 11.6 %scatter_fusion = bf16[64,2,128,128]{3,2,1,0:T(8,128)(2,1)} fusion(bf16[64,2,128,128]{3,2,1,0:T(8,128)(2,1)} %broadcast_in_dim.8, s32[56]{0:T(128)S(1)} %fusion.13, bf16[56,2,128,128]{3,2,1,0:T(8,128)(2,1)} %bitcast.79), kind=kCustom, calls=%fused_computation.1 | custom fusion | bytes 11010272 | tf_op jit(solution)/shard_map/scatter | solution.py:44
  146.4 322.6 %all_to_all.10 = bf16[32,2,2,128,128]{4,3,2,1,0:T(8,128)(2,1)S(1)} all-to-all(bf16[32,2,2,128,128]{4,3,2,1,0:T(8,128)(2,1)} %bitcast.78), channel_id=1, replica_groups=mesh['dp'=32,'tensor'=16] {'dp'}, dimensions={0} | all-to-all | bytes 8388608 | tf_op jit(solution)/shard_map/all_to_all | solution.py:45
  469.0 1.5 convert_reduce_fusion
  (4 shorter events, 0.0 us)
Async XLA Ops:
  0.0 112.7 %copy-start = (bf16[7,8,128,128]{3,2,1,0:T(8,128)(2,1)S(1)}, bf16[7,8,128,128]{3,2,1,0:T(8,128)(2,1)}, u32[]{:S(2)}) copy-start(bf16[7,8,128,128]{3,2,1,0:T(8,128)(2,1)} %param.8) | copy-start | bytes 5505028
  3.6 18.3 %copy-start.4 = (s32[7,8]{1,0:T(8,128)S(1)}, s32[7,8]{1,0:T(8,128)}, u32[]{:S(2)}) copy-start(s32[7,8]{1,0:T(8,128)} %param.10) | copy-start | bytes 676
  3.6 95.2 %all-to-all-start = ((bf16[16,512,256]{1,2,0:T(8,128)(2,1)}), bf16[16,512,256]{1,2,0:T(8,128)(2,1)}, u32[]{:S(2)}, u32[]{:S(2)}) async-start(bf16[16,512,256]{1,2,0:T(8,128)(2,1)} %stack.8), calls=%async_computation | async-start | bytes 8388608 | tf_op jit(solution)/shard_map/all_to_all | solution.py:14
  23.5 1.6 copy-start.3
  112.7 5.3 %copy-start.1 = (f32[512,7,128]{2,0,1:T(8,128)S(1)}, f32[512,7,128]{2,0,1:T(8,128)}, u32[]{:S(2)}) copy-start(f32[512,7,128]{2,0,1:T(8,128)} %copy.18) | copy-start | bytes 5505028
  112.7 5.8 %copy-start.2 = (bf16[56,512,128]{2,1,0:T(8,128)(2,1)S(1)}, bf16[56,512,128]{2,1,0:T(8,128)(2,1)}, u32[]{:S(2)}) copy-start(bf16[56,512,128]{2,1,0:T(8,128)(2,1)} %gather_fusion) | copy-start | bytes 22020100
  118.0 1.6 copy-start.5
